TPU v7x, 32 devices: a whole 2x2x4 slice. The times are simulated.
32 devices in a mesh: rows: 8 (over z, x), seq: 4 (over y, core).
Axes of the slice: x: 2, y: 2, z: 4, core: 2. Of those that a mesh axis runs over, the one named last changes fastest.
Arguments:
- frames_in: bfloat16 [16, 4096, 512], P('rows', 'seq'), may hold values from -6 to 6
- lengths: int32 [16, 4], P('rows'), may hold values from 1 to 2048, 4096 in all within a row
- bw_ids: int32 [16, 4], P('rows'), may hold values from 0 to 3
- owner_list: int32 [137], replicated, may hold values from 0 to 7, as said below
- master: float32 [216, 32, 512], P('rows')
- moment1: float32 [216, 32, 512], P('rows')
- moment2: float32 [216, 32, 512], P('rows'), as said below
- wave_grad: bfloat16 [16, 1310720], P('rows', 'seq'), may hold values from -6 to 6
Outputs:
- waveform: float32 [16, 1310720], P('rows', 'seq')
- input_grad: float32 [16, 4096, 512], P('rows', 'seq')
- new_master: float32 [216, 32, 512], P('rows')
- new_moment1: float32 [216, 32, 512], P('rows')
- new_moment2: float32 [216, 32, 512], P('rows')
Inputs may be any that keep to these rules, and one draw needn't show every extreme that they name: `owner_list`: no index along rows owns more than 27 buckets, and some index owns exactly 27. `moment2`: every entry is positive.
All inputs are finite; a program needn't handle non-finite values.
Results may differ from a plain program's by a relative error of at most 0.012.
The roundings to bfloat16 on the way count: a program that leaves them out, or rounds other values in their place, can miss the bound.
Values may be sent and summed in bfloat16 or wider, within the bound.
No kernel may reach another device: no remote copies, remote signals or barrier semaphores. Data moves between devices by JAX's collectives and lax.ppermute only.
A program may use at most 192 MiB of HBM per device.

v0:
```python
import math
import jax
import jax.numpy as jnp
from jax import lax
from jax.sharding import PartitionSpec as P

FF = 1536
NFFT = 1280
HOP = 320
NBW = 4
KW = 7
UTT = 4
BR = 32
STEP_COUNT = 6
BINS = 641
NOUT = 1282
VROWS = 20
IN_ROWS = 3
HEAD_ROWS = 3
PR = 4380
NB = 137
NORM_EPS = 1e-06
ENV_FLOOR = 0.5
BETA_ONE = 0.8
BETA_TWO = 0.9
LEARN_RATE = 0.04
WEIGHT_DECAY = 0.01
ADAM_EPS = 1e-08


def padded(block, sides, width):
    for axis, dim in sides:
        count = lax.axis_size(axis)
        forward = [(i, i + 1) for i in range(count - 1)]
        backward = [(target, source) for source, target in forward]
        low = lax.ppermute(
            lax.slice_in_dim(block, block.shape[dim] - width, None, axis=dim), axis, forward
        )
        high = lax.ppermute(lax.slice_in_dim(block, 0, width, axis=dim), axis, backward)
        block = jnp.concatenate([low, block, high], axis=dim)
    return block


def from_behind(block, axis, distance):
    devices = range(lax.axis_size(axis))
    route = [(i - distance, i) for i in devices if i - distance in devices]
    return lax.ppermute(block, axis, route)


def slot_maps(owner_list, owner_count, slot_count):
    bucket_count = owner_list.shape[0]
    bucket_index = jnp.arange(bucket_count, dtype=jnp.int32)
    same_owner = owner_list[None, :] == owner_list[:, None]
    before = bucket_index[None, :] < bucket_index[:, None]
    slot_rank = jnp.sum((same_owner & before).astype(jnp.int32), axis=1)
    bucket_place = owner_list * slot_count + slot_rank
    targets = jnp.arange(owner_count * slot_count, dtype=jnp.int32)
    slot_match = bucket_place[None, :] == targets[:, None]
    found_bucket = jnp.sum(slot_match.astype(jnp.int32) * bucket_index[None, :], axis=1)
    source = jnp.where(jnp.any(slot_match, axis=1), found_bucket, bucket_count)
    return (bucket_place, source)


def synthesis_table():
    bin_index = jnp.arange(BINS, dtype=jnp.int32)[:, None]
    tap_index = jnp.arange(NFFT, dtype=jnp.int32)[None, :]
    turns = bin_index * tap_index % NFFT
    angle = turns.astype(jnp.float32) * (2.0 * math.pi / NFFT)
    edge_bin = (bin_index == 0) | (bin_index == NFFT // 2)
    factor = jnp.where(edge_bin, 1.0, 2.0).astype(jnp.float32) / NFFT
    return jnp.concatenate([factor * jnp.cos(angle), -factor * jnp.sin(angle)], axis=0)


def hann_window():
    angle = jnp.arange(NFFT, dtype=jnp.int32).astype(jnp.float32) * (2.0 * math.pi / NFFT)
    return 0.5 - 0.5 * jnp.cos(angle)


def segment_ids(lengths, first_index, span):
    starts = jnp.cumsum(lengths, axis=1) - lengths
    frame_index = first_index + jnp.arange(span, dtype=jnp.int32)
    return jnp.sum((starts[:, None, :] <= frame_index[None, :, None]).astype(jnp.int32), axis=2) - 1


def layer_norm(values):
    row_mean = jnp.mean(values, axis=-1, keepdims=True)
    centered = values - row_mean
    return centered * lax.rsqrt(jnp.mean(centered * centered, axis=-1, keepdims=True) + NORM_EPS)


def ada_norm(values, scale_rows, shift_rows):
    return layer_norm(values) * scale_rows + shift_rows


def final_norm(values, norm_gain, norm_bias):
    return layer_norm(values) * norm_gain[None, :] + norm_bias[None, :]


def exact_gelu(values):
    return jax.nn.gelu(values, approximate=False)


def contract(left_side, right_side, left_dim, right_dim):
    return lax.dot_general(
        left_side,
        right_side,
        (((left_dim,), (right_dim,)), ((), ())),
        preferred_element_type=jnp.float32,
    )


def local(frames_in, lengths, bw_ids, owner_list, master, moment1, moment2, wave_grad):
    rows_here, frames_here, channels = frames_in.shape
    slot_count = master.shape[0]
    frame_count = rows_here * frames_here
    lap_count = NFFT // HOP
    rim_width = (KW - 1) // 2
    margin = max(rim_width, lap_count - 1)
    bucket_place, source = slot_maps(owner_list, lax.axis_size("rows"), slot_count)
    gathered = lax.all_gather(master.astype(jnp.bfloat16), "rows", axis=0, tiled=True)
    buckets = jnp.take(gathered, bucket_place, axis=0)
    weight_table = buckets.reshape(-1, channels)[:PR]
    w_in = weight_table[:FF]
    w_out = weight_table[FF : 2 * FF]
    w_head = weight_table[2 * FF : 2 * FF + NOUT]
    row_start = 2 * FF + NOUT
    channel_rows = weight_table[row_start : row_start + VROWS].astype(jnp.float32)
    row_start = row_start + VROWS
    bias_in = weight_table[row_start : row_start + IN_ROWS].reshape(-1).astype(jnp.float32)
    row_start = row_start + IN_ROWS
    bias_head = (
        weight_table[row_start : row_start + HEAD_ROWS].reshape(-1)[:NOUT].astype(jnp.float32)
    )
    conv_weight = channel_rows[:KW]
    conv_bias = channel_rows[KW]
    ada_scale = channel_rows[KW + 1 : KW + 1 + NBW]
    ada_shift = channel_rows[KW + 1 + NBW : KW + 1 + 2 * NBW]
    vec_base = KW + 1 + 2 * NBW
    bias_out = channel_rows[vec_base]
    layer_scale = channel_rows[vec_base + 1]
    norm_gain = channel_rows[vec_base + 2]
    norm_bias = channel_rows[vec_base + 3]
    first_index = lax.axis_index("seq") * frames_here - margin
    segment = segment_ids(lengths, first_index, frames_here + 2 * margin)
    own_segment = segment[:, margin : margin + frames_here]
    halo_frames = padded(frames_in, (("seq", 1),), rim_width)
    wide_frames = halo_frames.astype(jnp.float32)
    conv_keep = []
    conv_out = jnp.zeros((rows_here, frames_here, channels), jnp.float32) + conv_bias
    for tap_index in range(KW):
        lower = margin - rim_width + tap_index
        keep = (segment[:, lower : lower + frames_here] == own_segment).astype(jnp.float32)[
            :, :, None
        ]
        conv_keep.append(keep)
        conv_out = (
            conv_out
            + keep * wide_frames[:, tap_index : tap_index + frames_here] * conv_weight[tap_index]
        )
    conv_out = conv_out.reshape(frame_count, channels)
    utt_pick = (own_segment[:, :, None] == jnp.arange(UTT, dtype=jnp.int32)[None, None, :]).astype(
        jnp.int32
    )
    frame_ids = jnp.sum(utt_pick * bw_ids[:, None, :], axis=2).reshape(frame_count)
    bw_onehot = (frame_ids[:, None] == jnp.arange(NBW, dtype=jnp.int32)[None, :]).astype(
        jnp.float32
    )
    scale_rows = jnp.dot(bw_onehot, ada_scale, precision=lax.Precision.HIGHEST)
    shift_rows = jnp.dot(bw_onehot, ada_shift, precision=lax.Precision.HIGHEST)
    ada_value, ada_back = jax.vjp(ada_norm, conv_out, scale_rows, shift_rows)
    ada_low = ada_value.astype(jnp.bfloat16)
    hidden_pre = contract(ada_low, w_in, 1, 1) + bias_in[None, :]
    act_value, gelu_back = jax.vjp(exact_gelu, hidden_pre)
    act_low = act_value.astype(jnp.bfloat16)
    branch = contract(act_low, w_out, 1, 0) + bias_out[None, :]
    frames_flat = frames_in.reshape(frame_count, channels).astype(jnp.float32)
    residual = frames_flat + layer_scale[None, :] * branch
    normed_value, final_back = jax.vjp(final_norm, residual, norm_gain, norm_bias)
    normed_low = normed_value.astype(jnp.bfloat16)
    head_out = contract(normed_low, w_head, 1, 1) + bias_head[None, :]
    magnitude = jnp.exp(head_out[:, :BINS])
    phase_angle = head_out[:, BINS:]
    real_part = magnitude * jnp.cos(phase_angle)
    imag_part = magnitude * jnp.sin(phase_angle)
    spectrum_low = jnp.concatenate([real_part, imag_part], axis=1).astype(jnp.bfloat16)
    synthesis = synthesis_table().astype(jnp.bfloat16)
    signal = contract(spectrum_low, synthesis, 1, 0)
    window_rows = hann_window().reshape(lap_count, HOP)
    pieces = signal.reshape(rows_here, frames_here, lap_count, HOP) * window_rows[None, None, :, :]
    lap_keep = []
    numerator = jnp.zeros((rows_here, frames_here + lap_count - 1, HOP), jnp.float32)
    envelope = jnp.zeros((rows_here, frames_here, HOP), jnp.float32)
    for lap_index in range(lap_count):
        ahead = margin + lap_index
        keep = (segment[:, ahead : ahead + frames_here] == own_segment).astype(jnp.float32)[
            :, :, None
        ]
        lap_keep.append(keep)
        numerator = numerator + jnp.pad(
            keep * pieces[:, :, lap_index], ((0, 0), (lap_index, lap_count - 1 - lap_index), (0, 0))
        )
        behind = margin - lap_index
        back_keep = (segment[:, behind : behind + frames_here] == own_segment).astype(jnp.float32)[
            :, :, None
        ]
        envelope = envelope + back_keep * (window_rows[lap_index] ** 2)[None, None, :]
    arrived = from_behind(numerator[:, frames_here:], "seq", 1)
    numerator = numerator[:, :frames_here] + jnp.pad(
        arrived, ((0, 0), (0, frames_here - lap_count + 1), (0, 0))
    )
    denominator = jnp.maximum(envelope, ENV_FLOOR)
    waveform = (numerator / denominator).reshape(rows_here, frames_here * HOP)
    scaled = wave_grad.astype(jnp.float32).reshape(rows_here, frames_here, HOP) / denominator
    later_rows = from_behind(scaled[:, : lap_count - 1], "seq", -1)
    reach_rows = jnp.concatenate([scaled, later_rows], axis=1)
    signal_grad = jnp.stack(
        [
            lap_keep[lap_index]
            * window_rows[lap_index][None, None, :]
            * reach_rows[:, lap_index : lap_index + frames_here]
            for lap_index in range(lap_count)
        ],
        axis=2,
    )
    signal_low = signal_grad.reshape(frame_count, NFFT).astype(jnp.bfloat16)
    spec_grad = contract(signal_low, synthesis, 1, 1)
    real_grad = spec_grad[:, :BINS]
    imag_grad = spec_grad[:, BINS:]
    head_grad = jnp.concatenate(
        [
            real_grad * real_part + imag_grad * imag_part,
            imag_grad * real_part - real_grad * imag_part,
        ],
        axis=1,
    ).astype(jnp.bfloat16)
    grad_w_head = contract(head_grad, normed_low, 0, 0)
    grad_b_head = jnp.sum(head_grad, axis=0, dtype=jnp.float32)
    normed_grad = contract(head_grad, w_head, 1, 0)
    residual_grad, grad_gain, grad_bias = final_back(normed_grad)
    branch_low = (layer_scale[None, :] * residual_grad).astype(jnp.bfloat16)
    grad_layer_scale = jnp.sum(residual_grad * branch, axis=0)
    grad_w_out = contract(act_low, branch_low, 0, 0)
    grad_b_out = jnp.sum(branch_low, axis=0, dtype=jnp.float32)
    act_grad = contract(branch_low, w_out, 1, 1)
    pre_low = gelu_back(act_grad)[0].astype(jnp.bfloat16)
    grad_w_in = contract(pre_low, ada_low, 0, 0)
    grad_b_in = jnp.sum(pre_low, axis=0, dtype=jnp.float32)
    ada_grad = contract(pre_low, w_in, 1, 0)
    conv_grad, scale_grad_rows, shift_grad_rows = ada_back(ada_grad)
    grad_scales = lax.dot_general(
        bw_onehot, scale_grad_rows, (((0,), (0,)), ((), ())), precision=lax.Precision.HIGHEST
    )
    grad_shifts = lax.dot_general(
        bw_onehot, shift_grad_rows, (((0,), (0,)), ((), ())), precision=lax.Precision.HIGHEST
    )
    conv_rows = conv_grad.reshape(rows_here, frames_here, channels)
    grad_conv_b = jnp.sum(conv_grad, axis=0)
    grad_conv_w = jnp.stack(
        [
            jnp.sum(
                conv_keep[tap_index]
                * conv_rows
                * wide_frames[:, tap_index : tap_index + frames_here],
                axis=(0, 1),
            )
            for tap_index in range(KW)
        ],
        axis=0,
    )
    halo_grad = padded(conv_rows, (("seq", 1),), rim_width)
    input_grad = residual_grad.reshape(rows_here, frames_here, channels)
    for tap_index in range(KW):
        lower = margin + rim_width - tap_index
        keep = (segment[:, lower : lower + frames_here] == own_segment).astype(jnp.float32)[
            :, :, None
        ]
        begin = 2 * rim_width - tap_index
        input_grad = (
            input_grad + conv_weight[tap_index] * keep * halo_grad[:, begin : begin + frames_here]
        )
    vec_grads = jnp.concatenate(
        [
            grad_conv_w,
            grad_conv_b[None, :],
            grad_scales,
            grad_shifts,
            jnp.stack([grad_b_out, grad_layer_scale, grad_gain, grad_bias], axis=0),
        ],
        axis=0,
    )
    in_rows = grad_b_in.reshape(IN_ROWS, channels)
    head_rows = jnp.pad(grad_b_head, (0, HEAD_ROWS * channels - NOUT)).reshape(HEAD_ROWS, channels)
    grad_table = jnp.concatenate(
        [grad_w_in, grad_w_out, grad_w_head, vec_grads, in_rows, head_rows], axis=0
    )
    grad_buckets = jnp.pad(grad_table, ((0, NB * BR - PR), (0, 0))).reshape(NB, BR, channels)
    empty_bucket = jnp.zeros((1, BR, channels), jnp.float32)
    summed = lax.psum(grad_buckets, ("rows", "seq"))
    extended = jnp.concatenate([summed, empty_bucket], axis=0)
    my_sources = lax.dynamic_slice_in_dim(source, lax.axis_index("rows") * slot_count, slot_count)
    reduced = jnp.take(extended, my_sources, axis=0)
    first_new = BETA_ONE * moment1 + (1.0 - BETA_ONE) * reduced
    second_new = BETA_TWO * moment2 + (1.0 - BETA_TWO) * reduced * reduced
    first_fix = 1.0 - BETA_ONE**STEP_COUNT
    second_fix = 1.0 - BETA_TWO**STEP_COUNT
    master_new = master - LEARN_RATE * (
        first_new / first_fix / (jnp.sqrt(second_new / second_fix) + ADAM_EPS)
        + WEIGHT_DECAY * master
    )
    return (waveform, input_grad, master_new, first_new, second_new)


def solution(mesh):
    in_specs = (
        P("rows", "seq", None),
        P("rows", None),
        P("rows", None),
        P(),
        P("rows", None, None),
        P("rows", None, None),
        P("rows", None, None),
        P("rows", "seq"),
    )
    out_specs = (
        P("rows", "seq"),
        P("rows", "seq", None),
        P("rows", None, None),
        P("rows", None, None),
        P("rows", None, None),
    )
    return jax.shard_map(local, mesh=mesh, in_specs=in_specs, out_specs=out_specs, check_vma=False)
```

profile of v0, /device:TPU:0, one launch (start us, length us, event | category | flops | bytes accessed | tf_op | source)
XLA Modules:
  0.0 546.3 jit_solution(15566940357598605938)
XLA Ops:
  7.2 2.5 convert_element_type.160
  15.8 2.7 reshape.271
  21.1 2.9 fusion.48
  26.2 2.7 reshape.270
  33.0 2.8 fusion.47
  35.9 15.2 %multiply_convert_fusion.2 = (bf16[641,1280]{1,0:T(8,128)(2,1)}, bf16[641,1280]{1,0:T(8,128)(2,1)}) fusion(f32[641]{0:T(1024)S(1)} %fusion.74, f32[641]{0:T(1024)S(1)} %select_multiply_fusion), kind=kLoop, calls=%fused_computation.89 | loop fusion | flops 10666240 | bytes 3287048 | tf_op jit(solution)/shard_map/convert.12
  51.9 9.4 %concatenate.35 = bf16[2,1030,512]{2,1,0:T(8,128)(2,1)S(1)} concatenate(bf16[2,3,512]{2,1,0:T(4,128)(2,1)S(1)} %collective-permute-done, bf16[2,1024,512]{2,1,0:T(8,128)(2,1)} %param.8, bf16[2,3,512]{2,1,0:T(4,128)(2,1)S(1)} %collective-permute-done.1), dimensions={1} | concatenate | bytes 4218880 | tf_op jit(solution)/shard_map/concatenate | solution.py:40
  61.3 2.6 convert_element_type.164
  63.8 4.7 fusion.55
  68.5 3.2 pad_maximum_fusion.1
  71.7 10.2 %copy.40 = bf16[2,1024,4,320]{1,0,3,2:T(2,128)(2,1)} copy(bf16[2,1024,4,320]{1,3,0,2:T(8,128)(2,1)} %pad_maximum_fusion.1) | data formatting | bytes 10485760 | tf_op jit(solution)/shard_map/stack | solution.py:216
  81.9 4.8 copy.45
  86.7 9.7 %fusion.49 = f32[2048,1282]{0,1:T(8,128)} fusion(bf16[2048,1280]{0,1:T(8,128)(2,1)S(1)} %bitcast.122, bf16[641,1280]{1,0:T(8,128)(2,1)S(1)} %copy-done.20, bf16[641,1280]{1,0:T(8,128)(2,1)S(1)} %copy-done.21), kind=kOutput, calls=%fused_computation.122 | convolution fusion | flops 6727936000 | bytes 19026944 | tf_op jit(solution)/shard_map/dot_general | solution.py:104
  96.5 25.9 %all-gather.2.cloned.1.call-done = bf16[216,32,512]{2,1,0:T(8,128)(2,1)} async-done(((bf16[27,32,512]{2,1,0:T(8,128)(2,1)}), bf16[216,32,512]{2,1,0:T(8,128)(2,1)}) %all-gather.2.cloned.1.call-update) | async-done | bytes 7077904 | tf_op jit(solution)/shard_map/all_gather | solution.py:120
  122.3 10.9 %gather_fusion = bf16[137,32,512]{2,1,0:T(8,128)(2,1)} fusion(bf16[216,32,512]{2,1,0:T(8,128)(2,1)} %all-gather.2.cloned.1.call-done, s32[1024]{0:T(1024)S(1)} %pad_clamp_fusion.1), kind=kCustom, calls=%fused_computation | custom fusion | bytes 8978980 | tf_op jit(solution)/shard_map/jit(_take)/gather | solution.py:121
  133.3 4.1 bitcast_select_fusion
  137.5 2.6 broadcast_select_fusion
  140.2 2.4 slice-done
  142.7 6.1 %fusion.88 = (f32[2,1024]{1,0:T(2,128)S(1)}, f32[2,1024,512]{2,1,0:T(8,128)S(1)}) fusion(f32[512]{0:T(512)S(1)} %bitcast.134, f32[2,1030,512]{2,1,0:T(8,128)S(1)} %bitcast.114, f32[2,1024]{1,0:T(2,128)S(1)} %get-tuple-element.69, f32[512]{0:T(512)S(1)} %bitcast.136, f32[2,1024]{1,0:T(2,128)S(1)} %get-tuple-element.70, f32[512]{0:T(512)S(1)} %bitcast.138, ...), kind=kLoop, calls=%fused_computation.211 | loop fusion | flops 22018048 | bytes 33628160 | tf_op jit(solution)/shard_map/jvp()/reduce_sum | solution.py:86
  152.1 2.5 fusion.60
  157.8 4.0 add_convert_fusion.3
  161.8 31.4 %multiply_convert_fusion = (bf16[2048,1536]{1,0:T(8,128)(2,1)S(1)}, f32[2048,1536]{1,0:T(8,128)}, f32[2048,1536]{1,0:T(8,128)}) fusion(f32[1536]{0:T(1024)S(1)} %reshape.280, bf16[2048,512]{1,0:T(8,128)(2,1)S(1)} %add_convert_fusion.3, bf16[1536,512]{1,0:T(8,128)(2,1)S(1)} %bitcast.123), kind=kOutput, calls=%fused_computation.6 | convolution fusion | flops 3428843520 | bytes 35133440 | tf_op jit(solution)/shard_map/dot_general | solution.py:104
  193.2 5.6 %fusion.86 = (f32[2048]{0:T(1024)S(1)}, f32[2048,512]{1,0:T(8,128)S(1)}, f32[2048,512]{1,0:T(8,128)}) fusion(f32[512]{0:T(512)S(1)} %bitcast.159, f32[512]{0:T(512)S(1)} %bitcast.157, bf16[2,1024,512]{2,1,0:T(8,128)(2,1)S(1)} %copy-done.16, bf16[2048,1536]{1,0:T(8,128)(2,1)S(1)} %get-tuple-element.32, bf16[1536,512]{1,0:T(8,128)(2,1)S(1)} %bitcast.125), kind=kOutput, calls=%fused_computation.210 | convolution fusion | flops 3226466304 | bytes 18362368 | tf_op jit(solution)/shard_map/dot_general | solution.py:104
  201.6 5.8 %convolution_add_fusion = f32[2048,1282]{0,1:T(8,128)S(1)} fusion(f32[1282]{0:T(1024)S(1)} %slice_convert_fusion.1, bf16[4384,512]{1,0:T(8,128)(2,1)} %copy-done.13, f32[2048,512]{1,0:T(8,128)} %copy-done.8, f32[512]{0:T(512)S(1)} %bitcast.169, f32[512]{0:T(512)S(1)} %bitcast.163, f32[2048]{0:T(1024)S(1)} %fusion.70, f32[2048]{0:T(1024)S(1)} %broadcast_multiply_fusion), kind=kOutput, calls=%fused_computation.22 | convolution fusion | flops 2696417280 | bytes 16040968 | tf_op jit(solution)/shard_map/dot_general | solution.py:104
  207.5 24.2 %add_convert_fusion.1 = (bf16[2048,641]{0,1:T(8,128)(2,1)S(1)}, bf16[2048,641]{0,1:T(8,128)(2,1)S(1)}, bf16[2048,641]{0,1:T(8,128)(2,1)}, bf16[2048,641]{0,1:T(8,128)(2,1)}) fusion(f32[2048,1282]{0,1:T(8,128)} %fusion.49, f32[2048,1282]{0,1:T(8,128)S(1)} %convolution_add_fusion), kind=kLoop, calls=%fused_computation.31 | loop fusion | flops 15753216 | bytes 31506432 | tf_op jit(solution)/shard_map/convert.2
  233.9 6.2 %multiply_reduce_fusion = (f32[512]{0:T(512)S(1)}, f32[2048]{0:T(1024)S(1)}, f32[512]{0:T(512)S(1)}, f32[2048,512]{1,0:T(8,128)S(1)}) fusion(f32[2048,512]{1,0:T(8,128)S(1)} %copy-done.9, f32[2048]{0:T(1024)S(1)} %fusion.70, f32[2048]{0:T(1024)S(1)} %broadcast_multiply_fusion, f32[512]{0:T(512)S(1)} %bitcast.164, bf16[4384,512]{1,0:T(8,128)(2,1)} %copy-done.13, ...), kind=kOutput, calls=%fused_computation.64 | convolution fusion | flops 2707436544 | bytes 14989312 | tf_op jit(solution)/shard_map/dot_general | solution.py:104
  240.1 4.6 fusion.52
  249.5 3.6 fusion.95
  253.1 16.6 %convert_reduce_fusion = (f32[1536]{0:T(1024)S(1)}, bf16[2048,1536]{1,0:T(8,128)(2,1)}) fusion(f32[2048,1536]{1,0:T(8,128)} %get-tuple-element.33, bf16[2048,512]{1,0:T(8,128)(2,1)} %copy-done.19, bf16[1536,512]{1,0:T(8,128)(2,1)} %bitcast.126, f32[2048,1536]{1,0:T(8,128)} %get-tuple-element.84, f32[1536]{0:T(1024)S(1)} %reshape.280), kind=kOutput, calls=%fused_computation.4 | convolution fusion | flops 3274701312 | bytes 35139584 | tf_op jit(solution)/shard_map/dot_general | solution.py:104
  269.7 6.7 %multiply_reduce_fusion.9 = (f32[2048]{0:T(1024)S(1)}, f32[2048,512]{1,0:T(8,128)S(1)}) fusion(f32[2048,512]{1,0:T(8,128)S(1)} %copy-done.4, f32[2048,512]{1,0:T(8,128)S(1)} %copy-done.6, bf16[2048,1536]{1,0:T(8,128)(2,1)} %get-tuple-element.90, bf16[1536,512]{1,0:T(8,128)(2,1)} %bitcast.124), kind=kOutput, calls=%fused_computation.76 | convolution fusion | flops 3224369152 | bytes 20455424 | tf_op jit(solution)/shard_map/dot_general | solution.py:104
  276.4 5.1 fusion.94
  285.5 5.5 %fusion.84 = (f32[2048]{0:T(1024)S(1)}, f32[2048,512]{1,0:T(8,128)S(1)}) fusion(f32[2048]{0:T(1024)S(1)} %fusion.69, f32[2048]{0:T(1024)S(1)} %copy-done.39, f32[2048,512]{1,0:T(8,128)} %copy-done.7, f32[2048,512]{1,0:T(8,128)} %fusion.60, f32[2048]{0:T(1024)S(1)} %bitcast.132, f32[2,1024,512]{2,1,0:T(8,128)} %copy-done), kind=kLoop, calls=%fused_computation.208 | loop fusion | flops 7337984 | bytes 16809984 | tf_op jit(solution)/shard_map/transpose(jvp())/reduce_sum | solution.py:87
  291.5 3.2 slice-done.2
  294.7 5.3 multiply_reduce_fusion.2
  300.1 27.2 %concatenate.42 = f32[4380,512]{1,0:T(8,128)} concatenate(f32[1536,512]{1,0:T(8,128)} %fusion.94, f32[1536,512]{1,0:T(8,128)S(1)} %fusion.95, f32[1282,512]{1,0:T(8,128)} %fusion.52, f32[1,512]{1,0:T(1,128)S(1)} %bitcast.156, f32[1,512]{1,0:T(1,128)S(1)} %bitcast.155, f32[1,512]{1,0:T(1,128)S(1)} %bitcast.154, f32[1,512]{1,0:T(1,128)S(1)} %bitcast.153, f32[1,512]{1,0:T(1,128)S(1)} %bitcast.152, ...), dimensions={0} | concatenate | bytes 17940480 | tf_op jit(solution)/shard_map/concatenate | solution.py:293
  327.2 8.1 %pad.35 = f32[4384,512]{1,0:T(8,128)} pad(f32[4380,512]{1,0:T(8,128)} %concatenate.42, f32[]{:T(128)} %constant.72.clone.1), padding=0_4x0_0 | pad | bytes 17948676 | tf_op jit(solution)/shard_map/jit(_pad)/pad | solution.py:296
  337.1 13.9 %fusion.6 = f32[2048,1280]{0,1:T(8,128)} fusion(bf16[2048,641]{0,1:T(8,128)(2,1)} %get-tuple-element.41, bf16[2048,641]{0,1:T(8,128)(2,1)S(1)} %copy-done.15, bf16[641,1280]{1,0:T(8,128)(2,1)} %get-tuple-element.91, bf16[641,1280]{1,0:T(8,128)(2,1)} %get-tuple-element.92), kind=kOutput, calls=%fused_computation.34 | convolution fusion | flops 6738438144 | bytes 19018752 | tf_op jit(solution)/shard_map/dot_general | solution.py:104
  350.9 14.4 %reshape.268 = f32[2,1024,4,320]{1,0,3,2:T(2,128)} reshape(f32[2048,1280]{0,1:T(8,128)} %fusion.6) | data formatting | bytes 20971520 | tf_op jit(solution)/shard_map/reshape | solution.py:189
  365.4 8.5 %copy_multiply_fusion = f32[2,1024,4,320]{1,3,0,2:T(8,128)S(1)} fusion(f32[2,1024,4,320]{1,0,3,2:T(2,128)} %reshape.268, f32[4,320]{1,0:T(4,128)S(1)} %copy-done.52), kind=kLoop, calls=%fused_computation.21 | loop fusion | flops 2621440 | bytes 20976640 | tf_op jit(solution)/shard_map/mul | solution.py:189
  382.3 4.4 collective-permute-start.5
  386.8 2.4 fusion.43
  389.2 2.6 copy.36
  391.9 4.1 reshape.269
  396.1 20.3 %fusion.13 = f32[2,1024,512]{2,1,0:T(8,128)} fusion(f32[2,3,512]{2,1,0:T(4,128)S(1)} %collective-permute-done.5, f32[2,3,512]{2,1,0:T(4,128)S(1)} %collective-permute-done.4, f32[2,1024,512]{2,1,0:T(8,128)} %bitcast.119, f32[2,1024,512]{2,1,0:T(8,128)} %bitcast.118, f32[512]{0:T(512)S(1)} %bitcast.135, f32[2,1024]{1,0:T(2,128)S(1)} %copy-done.31, ...), kind=kLoop, calls=%fused_computation.46 | loop fusion | flops 27262976 | bytes 12670976 | tf_op jit(solution)/shard_map/add | solution.py:279
  416.3 103.8 %all-reduce.10.cloned.1.call-done = f32[137,32,512]{2,1,0:T(8,128)} async-done(((f32[137,32,512]{2,1,0:T(8,128)}), f32[137,32,512]{2,1,0:T(8,128)}) %all-reduce.10.cloned.1.call-update) | async-done | bytes 8978448 | tf_op jit(solution)/shard_map/psum | solution.py:298
  520.2 9.1 %concatenate.43 = f32[138,32,512]{2,1,0:T(8,128)} pad(f32[137,32,512]{2,1,0:T(8,128)} %all-reduce.10.cloned.1.call-done, f32[]{:T(128)} %constant.72.clone.1), padding=0_1x0_0x0_0 | pad | bytes 18022404 | tf_op jit(solution)/shard_map/concatenate | solution.py:299
  529.3 4.5 gather_fusion.1
  533.8 5.5 %multiply_subtract_fusion = (f32[27,32,512]{2,1,0:T(8,128)}, f32[27,32,512]{2,1,0:T(8,128)}, f32[27,32,512]{2,1,0:T(8,128)}) fusion(f32[27,32,512]{2,1,0:T(8,128)S(1)} %copy-done.12, f32[27,32,512]{2,1,0:T(8,128)S(1)} %gather_fusion.1, pred[27]{0:T(512)(128)(4,1)S(1)} %copy-done.68, f32[27,32,512]{2,1,0:T(8,128)} %param.13, f32[27,32,512]{2,1,0:T(8,128)} %param.14), kind=kLoop, calls=%fused_computation.127 | loop fusion | flops 7077888 | bytes 12386331 | tf_op jit(solution)/shard_map/sub | solution.py:306
  (236 shorter events, 46.5 us)
Async XLA Ops:
  7.2 115.2 %all-gather.2.cloned.1.call-start = ((), (), s32[]{:S(2)}) async-start(), calls=%async_computation | async-start | bytes 7962624 | tf_op jit(solution)/shard_map/all_gather | solution.py:120
  9.8 510.4 %all-reduce.10.cloned.1.call-start = ((), (), s32[]{:S(2)}) async-start(), calls=%async_computation.1 | async-start | bytes 17956864 | tf_op jit(solution)/shard_map/psum | solution.py:298
  10.6 41.3 %collective-permute-start = (bf16[2,3,512]{2,1,0:T(4,128)(2,1)S(1)}, bf16[2,3,512]{2,1,0:T(4,128)(2,1)S(1)}, u32[]{:S(2)}, u32[]{:S(2)}) collective-permute-start(bf16[2,3,512]{2,1,0:T(4,128)(2,1)S(1)} %get-tuple-element.55), channel_id=1, source_target_pairs={{0,1},{1,2},{2,3},{4,5},{5,6},{6,7},{8,9},{9,10},{10,11},{12,13},{... | collective-permute-start | bytes 18440 | tf_op jit(solution)/shard_map/ppermute | solution.py:36
  12.9 38.9 %collective-permute-start.1 = (bf16[2,3,512]{2,1,0:T(4,128)(2,1)S(1)}, bf16[2,3,512]{2,1,0:T(4,128)(2,1)S(1)}, u32[]{:S(2)}, u32[]{:S(2)}) collective-permute-start(bf16[2,3,512]{2,1,0:T(4,128)(2,1)S(1)} %get-tuple-element.54), channel_id=1, source_target_pairs={{1,0},{2,1},{3,2},{5,4},{6,5},{7,6},{9,8},{10,9},{11,10},{13,12},{... | collective-permute-start | bytes 18440 | tf_op jit(solution)/shard_map/ppermute | solution.py:39
  20.9 12.1 %copy-start.44 = (f32[320]{0:T(512)}, f32[320]{0:T(512)S(1)}, u32[]{:S(2)}) copy-start(f32[320]{0:T(512)S(1)} %get-tuple-element.75) | copy-start | bytes 3844
  20.9 12.1 %copy-start.46 = (f32[320]{0:T(512)}, f32[320]{0:T(512)S(1)}, u32[]{:S(2)}) copy-start(f32[320]{0:T(512)S(1)} %get-tuple-element.76) | copy-start | bytes 3844
  20.9 12.1 %copy-start.48 = (f32[320]{0:T(512)}, f32[320]{0:T(512)S(1)}, u32[]{:S(2)}) copy-start(f32[320]{0:T(512)S(1)} %get-tuple-element.77) | copy-start | bytes 3844
  20.9 12.1 %copy-start.50 = (f32[320]{0:T(512)}, f32[320]{0:T(512)S(1)}, u32[]{:S(2)}) copy-start(f32[320]{0:T(512)S(1)} %get-tuple-element.78) | copy-start | bytes 3844
  21.1 119.1 %copy-start.24 = (f32[2,1024]{1,0:T(2,128)}, f32[2,1024]{1,0:T(2,128)S(1)}, u32[]{:S(2)}) copy-start(f32[2,1024]{1,0:T(2,128)S(1)} %get-tuple-element.68) | copy-start | bytes 24580
  21.1 119.1 %copy-start.26 = (f32[2,1024]{1,0:T(2,128)}, f32[2,1024]{1,0:T(2,128)S(1)}, u32[]{:S(2)}) copy-start(f32[2,1024]{1,0:T(2,128)S(1)} %get-tuple-element.72) | copy-start | bytes 24580
  21.1 119.1 %copy-start.28 = (f32[2,1024]{1,0:T(2,128)}, f32[2,1024]{1,0:T(2,128)S(1)}, u32[]{:S(2)}) copy-start(f32[2,1024]{1,0:T(2,128)S(1)} %get-tuple-element.73) | copy-start | bytes 24580
  21.1 119.1 %copy-start.30 = (f32[2,1024]{1,0:T(2,128)}, f32[2,1024]{1,0:T(2,128)S(1)}, u32[]{:S(2)}) copy-start(f32[2,1024]{1,0:T(2,128)S(1)} %get-tuple-element.69) | copy-start | bytes 24580
  21.1 119.1 %copy-start.32 = (f32[2,1024]{1,0:T(2,128)}, f32[2,1024]{1,0:T(2,128)S(1)}, u32[]{:S(2)}) copy-start(f32[2,1024]{1,0:T(2,128)S(1)} %get-tuple-element.70) | copy-start | bytes 24580
  21.1 119.1 %copy-start.34 = (f32[2,1024]{1,0:T(2,128)}, f32[2,1024]{1,0:T(2,128)S(1)}, u32[]{:S(2)}) copy-start(f32[2,1024]{1,0:T(2,128)S(1)} %get-tuple-element.71) | copy-start | bytes 24580
  24.8 39.0 %collective-permute-start.3 = (f32[2,3,320]{1,2,0:T(8,128)}, f32[2,3,320]{1,2,0:T(8,128)}, u32[]{:S(2)}, u32[]{:S(2)}) collective-permute-start(f32[2,3,320]{1,2,0:T(8,128)} %slice.387), channel_id=1, source_target_pairs={{1,0},{2,1},{3,2},{5,4},{6,5},{7,6},{9,8},{10,9},{11,10},{13,12},{... | collective-permute-start | bytes 23048 | tf_op jit(solution)/shard_map/ppermute | solution.py:47
  26.2 6.7 %copy-start.69 = (s32[2,4]{1,0:T(2,128)S(1)}, s32[2,4]{1,0:T(2,128)}, u32[]{:S(2)}) copy-start(s32[2,4]{1,0:T(2,128)} %param.10) | copy-start | bytes 100
  51.8 105.1 %copy-start.36 = (s32[1,8,2,128]{3,1,2,0:T(8,128)}, s32[1,8,2,128]{3,1,2,0:T(8,128)S(1)}, u32[]{:S(2)}) copy-start(s32[1,8,2,128]{3,1,2,0:T(8,128)S(1)} %copy.53) | copy-start | bytes 24580
  137.4 14.7 %copy-start.13 = (bf16[4384,512]{1,0:T(8,128)(2,1)}, bf16[4384,512]{1,0:T(8,128)(2,1)S(1)}, u32[]{:S(2)}) copy-start(bf16[4384,512]{1,0:T(8,128)(2,1)S(1)} %bitcast_select_fusion) | copy-start | bytes 13467652
  137.4 5.3 slice-start
  137.5 5.2 slice-start.1
  140.1 8.7 %copy-start.53 = (f32[1,512]{1,0:T(1,128)}, f32[1,512]{1,0:T(1,128)S(1)}, u32[]{:S(2)}) copy-start(f32[1,512]{1,0:T(1,128)S(1)} %get-tuple-element.59) | copy-start | bytes 6148
  140.1 8.7 %copy-start.55 = (f32[1,512]{1,0:T(1,128)}, f32[1,512]{1,0:T(1,128)S(1)}, u32[]{:S(2)}) copy-start(f32[1,512]{1,0:T(1,128)S(1)} %get-tuple-element.60) | copy-start | bytes 6148
  140.1 8.7 %copy-start.57 = (f32[1,512]{1,0:T(1,128)}, f32[1,512]{1,0:T(1,128)S(1)}, u32[]{:S(2)}) copy-start(f32[1,512]{1,0:T(1,128)S(1)} %get-tuple-element.61) | copy-start | bytes 6148
  140.1 8.7 %copy-start.59 = (f32[1,512]{1,0:T(1,128)}, f32[1,512]{1,0:T(1,128)S(1)}, u32[]{:S(2)}) copy-start(f32[1,512]{1,0:T(1,128)S(1)} %get-tuple-element.62) | copy-start | bytes 6148
  140.2 8.7 %copy-start.61 = (f32[1,512]{1,0:T(1,128)}, f32[1,512]{1,0:T(1,128)S(1)}, u32[]{:S(2)}) copy-start(f32[1,512]{1,0:T(1,128)S(1)} %get-tuple-element.63) | copy-start | bytes 6148
  140.2 8.7 %copy-start.63 = (f32[1,512]{1,0:T(1,128)}, f32[1,512]{1,0:T(1,128)S(1)}, u32[]{:S(2)}) copy-start(f32[1,512]{1,0:T(1,128)S(1)} %get-tuple-element.64) | copy-start | bytes 6148
  140.2 8.7 %copy-start.65 = (f32[1,512]{1,0:T(1,128)}, f32[1,512]{1,0:T(1,128)S(1)}, u32[]{:S(2)}) copy-start(f32[1,512]{1,0:T(1,128)S(1)} %get-tuple-element.65) | copy-start | bytes 6148
  149.7 7.2 %copy-start.38 = (f32[2048]{0:T(1024)}, f32[2048]{0:T(1024)S(1)}, u32[]{:S(2)}) copy-start(f32[2048]{0:T(1024)S(1)} %bitcast_rsqrt_fusion) | copy-start | bytes 24580
  157.8 35.4 %copy-start.23 = (bf16[48,32,512]{2,1,0:T(8,128)(2,1)}, bf16[48,32,512]{2,1,0:T(8,128)(2,1)S(1)}, u32[]{:S(2)}) copy-start(bf16[48,32,512]{2,1,0:T(8,128)(2,1)S(1)} %get-tuple-element.45) | copy-start | bytes 4718596
  161.8 31.4 %copy-start.17 = (bf16[2048,512]{1,0:T(8,128)(2,1)}, bf16[2048,512]{1,0:T(8,128)(2,1)S(1)}, u32[]{:S(2)}) copy-start(bf16[2048,512]{1,0:T(8,128)(2,1)S(1)} %add_convert_fusion.3) | copy-start | bytes 6291460
  161.8 31.4 %copy-start.16 = (bf16[2,1024,512]{2,1,0:T(8,128)(2,1)S(1)}, bf16[2,1024,512]{2,1,0:T(8,128)(2,1)}, u32[]{:S(2)}) copy-start(bf16[2,1024,512]{2,1,0:T(8,128)(2,1)} %param.8) | copy-start | bytes 6291460
  193.2 5.6 %copy-start.71 = (bf16[2048,1536]{1,0:T(8,128)(2,1)}, bf16[2048,1536]{1,0:T(8,128)(2,1)S(1)}, u32[]{:S(2)}) copy-start(bf16[2048,1536]{1,0:T(8,128)(2,1)S(1)} %get-tuple-element.32) | copy-start | bytes 18874372
  247.5 5.6 %copy-start.5 = (f32[2048,512]{1,0:T(8,128)}, f32[2048,512]{1,0:T(8,128)S(1)}, u32[]{:S(2)}) copy-start(f32[2048,512]{1,0:T(8,128)S(1)} %get-tuple-element.21) | copy-start | bytes 12582916
  253.1 16.6 %copy-start.4 = (f32[2048,512]{1,0:T(8,128)S(1)}, f32[2048,512]{1,0:T(8,128)}, u32[]{:S(2)}) copy-start(f32[2048,512]{1,0:T(8,128)} %bitcast_subtract_fusion) | copy-start | bytes 12582916
  253.1 16.6 %copy-start.6 = (f32[2048,512]{1,0:T(8,128)S(1)}, f32[2048,512]{1,0:T(8,128)}, u32[]{:S(2)}) copy-start(f32[2048,512]{1,0:T(8,128)} %fusion.60) | copy-start | bytes 12582916
  269.7 6.7 %copy-start.18 = (bf16[2048,512]{1,0:T(8,128)(2,1)S(1)}, bf16[2048,512]{1,0:T(8,128)(2,1)}, u32[]{:S(2)}) copy-start(bf16[2048,512]{1,0:T(8,128)(2,1)} %copy-done.17) | copy-start | bytes 6291460
  269.7 6.7 %copy-start.70 = (bf16[2048,1536]{1,0:T(8,128)(2,1)S(1)}, bf16[2048,1536]{1,0:T(8,128)(2,1)}, u32[]{:S(2)}) copy-start(bf16[2048,1536]{1,0:T(8,128)(2,1)} %get-tuple-element.90) | copy-start | bytes 18874372
  276.4 7.3 %copy-start.7 = (f32[2048,512]{1,0:T(8,128)}, f32[2048,512]{1,0:T(8,128)S(1)}, u32[]{:S(2)}) copy-start(f32[2048,512]{1,0:T(8,128)S(1)} %get-tuple-element.88) | copy-start | bytes 12582916
  291.5 8.6 %copy-start.2 = (f32[2048,512]{1,0:T(8,128)}, f32[2048,512]{1,0:T(8,128)S(1)}, u32[]{:S(2)}) copy-start(f32[2048,512]{1,0:T(8,128)S(1)} %get-tuple-element.25) | copy-start | bytes 12582916
  350.9 14.4 %copy-start.52 = (f32[4,320]{1,0:T(4,128)S(1)}, f32[4,320]{1,0:T(4,128)}, u32[]{:S(2)}) copy-start(f32[4,320]{1,0:T(4,128)} %multiply_subtract_fusion.2) | copy-start | bytes 15364
  376.4 10.4 %copy-start.45 = (f32[320]{0:T(512)S(1)}, f32[320]{0:T(512)}, u32[]{:S(2)}) copy-start(f32[320]{0:T(512)} %copy-done.44) | copy-start | bytes 3844
  376.4 10.4 %copy-start.47 = (f32[320]{0:T(512)S(1)}, f32[320]{0:T(512)}, u32[]{:S(2)}) copy-start(f32[320]{0:T(512)} %copy-done.46) | copy-start | bytes 3844
  376.4 10.4 %copy-start.49 = (f32[320]{0:T(512)S(1)}, f32[320]{0:T(512)}, u32[]{:S(2)}) copy-start(f32[320]{0:T(512)} %copy-done.48) | copy-start | bytes 3844
  376.4 10.4 %copy-start.51 = (f32[320]{0:T(512)S(1)}, f32[320]{0:T(512)}, u32[]{:S(2)}) copy-start(f32[320]{0:T(512)} %copy-done.50) | copy-start | bytes 3844
  376.4 10.3 %collective-permute-start.2 = (f32[2,3,320]{1,2,0:T(8,128)S(1)}, f32[2,3,320]{1,2,0:T(8,128)S(1)}, u32[]{:S(2)}, u32[]{:S(2)}) collective-permute-start(f32[2,3,320]{1,2,0:T(8,128)S(1)} %pad_add_fusion.1), channel_id=1, source_target_pairs={{0,1},{1,2},{2,3},{4,5},{5,6},{6,7},{8,9},{9,10},{10,11},{12,13},{... | collective-permute-start | bytes 23048 | tf_op jit(solution)/shard_map/ppermute | solution.py:47
  381.1 14.9 %collective-permute-start.4 = (f32[2,3,512]{2,1,0:T(4,128)S(1)}, f32[2,3,512]{2,1,0:T(4,128)S(1)}, u32[]{:S(2)}, u32[]{:S(2)}) collective-permute-start(f32[2,3,512]{2,1,0:T(4,128)S(1)} %get-tuple-element.49), channel_id=1, source_target_pairs={{1,0},{2,1},{3,2},{5,4},{6,5},{7,6},{9,8},{10,9},{11,10},{13,12},{... | collective-permute-start | bytes 36872 | tf_op jit(solution)/shard_map/ppermute | solution.py:39
  382.3 13.6 %collective-permute-start.5 = (f32[2,3,512]{2,1,0:T(4,128)S(1)}, f32[2,3,512]{2,1,0:T(4,128)S(1)}, u32[]{:S(2)}, u32[]{:S(2)}) collective-permute-start(f32[2,3,512]{2,1,0:T(4,128)S(1)} %get-tuple-element.50), channel_id=1, source_target_pairs={{0,1},{1,2},{2,3},{4,5},{5,6},{6,7},{8,9},{9,10},{10,11},{12,13},{... | collective-permute-start | bytes 36872 | tf_op jit(solution)/shard_map/ppermute | solution.py:36
  416.3 117.4 %copy-start.68 = (pred[27]{0:T(512)(128)(4,1)S(1)}, pred[27]{0:T(512)(128)(4,1)}, u32[]{:S(2)}) copy-start(pred[27]{0:T(512)(128)(4,1)} %get-tuple-element.18) | copy-start | bytes 85
  (38 other events, 134.6 us)
Sparse Core Ops, SparseCore 0:
  10.8 111.5 all-gather.1
  335.5 184.6 all-reduce.9
where the time goes:
time: 556 us; the launch traced here: 546 us
  other arithmetic  136 us (24%)
  local copies, waits for them, and re-layouts  133 us (24%)
  waiting for transfers between devices  130 us (23%)
  matrix products  119 us (21%)
  between operations  15.7 us (3%)
  starting transfers between devices  12.2 us (2%)
    dot_general x11, matrix products, contract(): lax.dot_general(left_side, right_side, (((left_dim,), (right_dim,)), ((),...  109 us
    psum x1, waiting for transfers between devices, local(): summed = lax.psum(grad_buckets, ('rows', 'seq'))  104 us
    another operation x3, other arithmetic  42.2 us
    concatenate x1, local copies, waits for them, and re-layouts, local(): jnp.concatenate([grad_w_in, grad_w_out, grad_w_head, vec_grads, in_rows,...  27.2 us
    all_gather x1, waiting for transfers between devices, local(): lax.all_gather(master.astype(jnp.bfloat16), 'rows', axis=0, tiled=True)  25.9 us
    add x1, other arithmetic, local(): input_grad + conv_weight[tap_index] * keep * halo_grad[:, begin:begin + f...  20.3 us
    unnamed x159, local copies, waits for them, and re-layouts  17.5 us
    reshape x1, local copies, waits for them, and re-layouts, local(): signal.reshape(rows_here, frames_here, lap_count, HOP)  14.4 us
  transfers between devices with their start and end apart: 8, of which 2 were waited for; matrix products, arithmetic and copies ran while one was open for 28% of the time, Pallas kernels for 0%

commit v1 on v0

--- a/solution.py
+++ b/solution.py
@@ -28,6 +28,18 @@
 ADAM_EPS = 1e-08
 
 
+def gather_by_bits(array, axis, dim):
+    ways, here = (lax.axis_size(axis), lax.axis_index(axis))
+    grown, reach = (array, 1)
+    while reach < ways:
+        theirs = lax.ppermute(grown, axis, [(d, d ^ reach) for d in range(ways)])
+        mine_first = jnp.concatenate([grown, theirs], axis=dim)
+        theirs_first = jnp.concatenate([theirs, grown], axis=dim)
+        grown = jnp.where(here & reach == 0, mine_first, theirs_first)
+        reach = 2 * reach
+    return grown
+
+
 def padded(block, sides, width):
     for axis, dim in sides:
         count = lax.axis_size(axis)
@@ -117,7 +129,7 @@
     rim_width = (KW - 1) // 2
     margin = max(rim_width, lap_count - 1)
     bucket_place, source = slot_maps(owner_list, lax.axis_size("rows"), slot_count)
-    gathered = lax.all_gather(master.astype(jnp.bfloat16), "rows", axis=0, tiled=True)
+    gathered = gather_by_bits(master.astype(jnp.bfloat16), "rows", 0)
     buckets = jnp.take(gathered, bucket_place, axis=0)
     weight_table = buckets.reshape(-1, channels)[:PR]
     w_in = weight_table[:FF]

time: 556 us -> 682 us (1.23)
  waiting for transfers between devices: 130 us -> 223 us
  other arithmetic: 136 us -> 150 us
  starting transfers between devices: 12.2 us -> 23.6 us
  local copies, waits for them, and re-layouts: 133 us -> 141 us
    ppermute x0 -> x3, waiting for transfers between devices: none -> 117 us  [gather_by_bits(): theirs = lax.ppermute(grown, axis, [(d, d ^ reach) for d in range(ways)])]
    all_gather x1 -> x0, waiting for transfers between devices: 25.9 us -> none  [local(): lax.all_gather(master.astype(jnp.bfloat16), 'rows', axis=0, tiled=True)]
    select_n x0 -> x3, other arithmetic: none -> 10.1 us  [gather_by_bits(): grown = jnp.where(here & reach == 0, mine_first, theirs_first)]
    ppermute x0 -> x3, starting transfers between devices: none -> 7.23 us  [gather_by_bits(): theirs = lax.ppermute(grown, axis, [(d, d ^ reach) for d in range(ways)])]
    unnamed x159 -> x183, local copies, waits for them, and re-layouts: 17.5 us -> 18.9 us
  transfers between devices with their start and end apart: 8 -> 10, of which waited for: 2 -> 3; matrix products, arithmetic and copies ran while one was open for 28% -> 25% of each run, Pallas kernels for 0% -> 0%
where the time goes in v1:
time: 682 us; the launch traced here: 672 us
  waiting for transfers between devices  223 us (33%)
  other arithmetic  150 us (22%)
  local copies, waits for them, and re-layouts  141 us (21%)
  matrix products  119 us (17%)
  starting transfers between devices  23.6 us (3%)
  between operations  15.7 us (2%)
    ppermute x3, waiting for transfers between devices, gather_by_bits(): theirs = lax.ppermute(grown, axis, [(d, d ^ reach) for d in range(ways)])  117 us
    dot_general x11, matrix products, contract(): lax.dot_general(left_side, right_side, (((left_dim,), (right_dim,)), ((),...  109 us
    psum x1, waiting for transfers between devices, local(): summed = lax.psum(grad_buckets, ('rows', 'seq'))  106 us
    another operation x3, other arithmetic  41.5 us
    concatenate x1, local copies, waits for them, and re-layouts, local(): jnp.concatenate([grad_w_in, grad_w_out, grad_w_head, vec_grads, in_rows,...  27.3 us
    add x1, other arithmetic, local(): input_grad + conv_weight[tap_index] * keep * halo_grad[:, begin:begin + f...  20.7 us
    unnamed x183, local copies, waits for them, and re-layouts  18.9 us
    reshape x1, local copies, waits for them, and re-layouts, local(): signal.reshape(rows_here, frames_here, lap_count, HOP)  14.4 us
  transfers between devices with their start and end apart: 10, of which 3 were waited for; matrix products, arithmetic and copies ran while one was open for 25% of the time, Pallas kernels for 0%

profile of v1, /device:TPU:0, one launch (start us, length us, event | category | flops | bytes accessed | tf_op | source)
XLA Modules:
  0.0 671.7 jit_solution(8410640900672271529)
XLA Ops:
  7.2 2.5 convert_element_type.160
  9.7 2.9 collective-permute-start
  19.8 2.7 reshape.271
  25.4 2.7 fusion.48
  30.9 2.7 reshape.270
  43.2 34.7 %collective-permute-done.1 = bf16[54,32,512]{2,1,0:T(8,128)(2,1)S(1)} collective-permute-done((bf16[54,32,512]{2,1,0:T(8,128)(2,1)S(1)}, bf16[54,32,512]{2,1,0:T(8,128)(2,1)S(1)}, u32[]{:S(2)}, u32[]{:S(2)}) %collective-permute-start.1) | collective-permute-done | bytes 1769504 | tf_op jit(solution)/shard_map/ppermute | solution.py:35
  78.5 2.7 collective-permute-start.2
  82.6 15.2 %multiply_convert_fusion.2 = (bf16[641,1280]{1,0:T(8,128)(2,1)}, bf16[641,1280]{1,0:T(8,128)(2,1)}) fusion(f32[641]{0:T(1024)S(1)} %fusion.74, f32[641]{0:T(1024)S(1)} %select_multiply_fusion), kind=kLoop, calls=%fused_computation.91 | loop fusion | flops 10666240 | bytes 3287048 | tf_op jit(solution)/shard_map/convert.12
  101.0 13.6 %concatenate.59 = bf16[2,1030,512]{2,1,0:T(8,128)(2,1)} concatenate(bf16[2,3,512]{2,1,0:T(4,128)(2,1)} %collective-permute-done.3, bf16[2,1024,512]{2,1,0:T(8,128)(2,1)} %param.8, bf16[2,3,512]{2,1,0:T(4,128)(2,1)} %collective-permute-done.4), dimensions={1} | concatenate | bytes 4218880 | tf_op jit(solution)/shard_map/concatenate | solution.py:52
  114.6 4.3 convert_element_type.164
  119.0 4.7 fusion.55
  123.8 3.2 pad_maximum_fusion.1
  126.9 10.2 %copy.34 = bf16[2,1024,4,320]{1,0,3,2:T(2,128)(2,1)} copy(bf16[2,1024,4,320]{1,3,0,2:T(8,128)(2,1)} %pad_maximum_fusion.1) | data formatting | bytes 10485760 | tf_op jit(solution)/shard_map/stack | solution.py:228
  137.2 4.8 copy.39
  142.0 9.7 %fusion.49 = f32[2048,1282]{0,1:T(8,128)} fusion(bf16[2048,1280]{0,1:T(8,128)(2,1)S(1)} %bitcast.122, bf16[641,1280]{1,0:T(8,128)(2,1)S(1)} %copy-done.22, bf16[641,1280]{1,0:T(8,128)(2,1)S(1)} %copy-done.23), kind=kOutput, calls=%fused_computation.124 | convolution fusion | flops 6727936000 | bytes 19026944 | tf_op jit(solution)/shard_map/dot_general | solution.py:116
  151.7 82.5 %collective-permute-done.2 = bf16[108,32,512]{2,1,0:T(8,128)(2,1)} collective-permute-done((bf16[108,32,512]{2,1,0:T(8,128)(2,1)S(1)}, bf16[108,32,512]{2,1,0:T(8,128)(2,1)}, u32[]{:S(2)}, u32[]{:S(2)}) %collective-permute-start.2) | collective-permute-done | bytes 3538976 | tf_op jit(solution)/shard_map/ppermute | solution.py:35
  234.2 7.1 %maximum_select_fusion = bf16[216,32,512]{2,1,0:T(8,128)(2,1)} fusion(bf16[108,32,512]{2,1,0:T(8,128)(2,1)} %collective-permute-done.2, bf16[108,32,512]{2,1,0:T(8,128)(2,1)S(1)} %maximum_select_fusion.1, pred[]{:T(512)S(6)} %eq.134), kind=kLoop, calls=%fused_computation.23 | loop fusion | flops 10616832 | bytes 14155777 | tf_op jit(solution)/shard_map/jit(_where)/select_n | solution.py:38
  241.3 10.7 %gather_fusion = bf16[137,32,512]{2,1,0:T(8,128)(2,1)} fusion(bf16[216,32,512]{2,1,0:T(8,128)(2,1)} %maximum_select_fusion, s32[1024]{0:T(1024)} %pad_clamp_fusion.1), kind=kCustom, calls=%fused_computation | custom fusion | bytes 8978980 | tf_op jit(solution)/shard_map/jit(_take)/gather | solution.py:133
  252.1 4.2 bitcast_select_fusion
  256.3 2.6 broadcast_select_fusion
  261.5 6.1 fusion.88
  271.0 2.5 fusion.60
  276.6 4.0 add_convert_fusion.3
  280.7 31.4 %multiply_convert_fusion = (bf16[2048,1536]{1,0:T(8,128)(2,1)S(1)}, f32[2048,1536]{1,0:T(8,128)}, f32[2048,1536]{1,0:T(8,128)}) fusion(f32[1536]{0:T(1024)S(1)} %reshape.280, bf16[2048,512]{1,0:T(8,128)(2,1)S(1)} %add_convert_fusion.3, bf16[1536,512]{1,0:T(8,128)(2,1)S(1)} %bitcast.123), kind=kOutput, calls=%fused_computation.6 | convolution fusion | flops 3428843520 | bytes 35133440 | tf_op jit(solution)/shard_map/dot_general | solution.py:116
  312.1 5.5 fusion.86
  320.5 5.8 convolution_add_fusion
  326.3 24.2 %add_convert_fusion.1 = (bf16[2048,641]{0,1:T(8,128)(2,1)S(1)}, bf16[2048,641]{0,1:T(8,128)(2,1)S(1)}, bf16[2048,641]{0,1:T(8,128)(2,1)}, bf16[2048,641]{0,1:T(8,128)(2,1)}) fusion(f32[2048,1282]{0,1:T(8,128)} %fusion.49, f32[2048,1282]{0,1:T(8,128)S(1)} %convolution_add_fusion), kind=kLoop, calls=%fused_computation.32 | loop fusion | flops 15753216 | bytes 31506432 | tf_op jit(solution)/shard_map/convert.2
  352.7 6.2 multiply_reduce_fusion
  358.9 4.6 fusion.52
  368.4 3.6 fusion.95
  372.0 16.5 %convert_reduce_fusion = (f32[1536]{0:T(1024)S(1)}, bf16[2048,1536]{1,0:T(8,128)(2,1)}) fusion(f32[2048,1536]{1,0:T(8,128)} %get-tuple-element.33, bf16[2048,512]{1,0:T(8,128)(2,1)} %copy-done.21, bf16[1536,512]{1,0:T(8,128)(2,1)} %bitcast.126, f32[2048,1536]{1,0:T(8,128)} %get-tuple-element.84, f32[1536]{0:T(1024)S(1)} %reshape.280), kind=kOutput, calls=%fused_computation.4 | convolution fusion | flops 3274701312 | bytes 35139584 | tf_op jit(solution)/shard_map/dot_general | solution.py:116
  388.5 6.7 multiply_reduce_fusion.9
  395.2 5.1 fusion.94
  404.3 5.5 fusion.84
  410.4 3.2 slice-done.2
  413.6 5.3 multiply_reduce_fusion.2
  418.9 27.3 %concatenate.66 = f32[4380,512]{1,0:T(8,128)} concatenate(f32[1536,512]{1,0:T(8,128)} %fusion.94, f32[1536,512]{1,0:T(8,128)S(1)} %fusion.95, f32[1282,512]{1,0:T(8,128)} %fusion.52, f32[1,512]{1,0:T(1,128)S(1)} %bitcast.156, f32[1,512]{1,0:T(1,128)S(1)} %bitcast.155, f32[1,512]{1,0:T(1,128)S(1)} %bitcast.154, f32[1,512]{1,0:T(1,128)S(1)} %bitcast.153, f32[1,512]{1,0:T(1,128)S(1)} %bitcast.152, ...), dimensions={0} | concatenate | bytes 17940480 | tf_op jit(solution)/shard_map/concatenate | solution.py:305
  446.2 8.1 %pad.35 = f32[4384,512]{1,0:T(8,128)} pad(f32[4380,512]{1,0:T(8,128)} %concatenate.66, f32[]{:T(128)} %constant.46.clone.1), padding=0_4x0_0 | pad | bytes 17948676 | tf_op jit(solution)/shard_map/jit(_pad)/pad | solution.py:308
  456.1 13.5 %fusion.6 = f32[2048,1280]{0,1:T(8,128)} fusion(bf16[2048,641]{0,1:T(8,128)(2,1)} %get-tuple-element.41, bf16[2048,641]{0,1:T(8,128)(2,1)S(1)} %copy-done.17, bf16[641,1280]{1,0:T(8,128)(2,1)} %get-tuple-element.91, bf16[641,1280]{1,0:T(8,128)(2,1)} %get-tuple-element.92), kind=kOutput, calls=%fused_computation.35 | convolution fusion | flops 6738438144 | bytes 19018752 | tf_op jit(solution)/shard_map/dot_general | solution.py:116
  469.6 14.4 %reshape.268 = f32[2,1024,4,320]{1,0,3,2:T(2,128)} reshape(f32[2048,1280]{0,1:T(8,128)} %fusion.6) | data formatting | bytes 20971520 | tf_op jit(solution)/shard_map/reshape | solution.py:201
  484.0 8.6 %copy_multiply_fusion = f32[2,1024,4,320]{1,3,0,2:T(8,128)S(1)} fusion(f32[2,1024,4,320]{1,0,3,2:T(2,128)} %reshape.268, f32[4,320]{1,0:T(4,128)S(1)} %copy-done.58), kind=kLoop, calls=%fused_computation.21 | loop fusion | flops 2621440 | bytes 20976640 | tf_op jit(solution)/shard_map/mul | solution.py:201
  502.1 7.9 %collective-permute-start.8 = (f32[2,3,512]{2,1,0:T(4,128)S(1)}, f32[2,3,512]{2,1,0:T(4,128)S(1)}, u32[]{:S(2)}, u32[]{:S(2)}) collective-permute-start(f32[2,3,512]{2,1,0:T(4,128)S(1)} %get-tuple-element.50), channel_id=1, source_target_pairs={{0,1},{1,2},{2,3},{4,5},{5,6},{6,7},{8,9},{9,10},{10,11},{12,13},{... | collective-permute-start | bytes 36872 | tf_op jit(solution)/shard_map/ppermute | solution.py:48
  514.8 4.1 reshape.269
  519.0 20.7 %fusion.13 = f32[2,1024,512]{2,1,0:T(8,128)} fusion(f32[2,3,512]{2,1,0:T(4,128)S(1)} %collective-permute-done.8, f32[2,3,512]{2,1,0:T(4,128)S(1)} %collective-permute-done.7, f32[2,1024,512]{2,1,0:T(8,128)} %bitcast.119, f32[2,1024,512]{2,1,0:T(8,128)} %bitcast.118, f32[512]{0:T(512)S(1)} %bitcast.135, f32[2,1024]{1,0:T(2,128)S(1)} %copy-done.36, ...), kind=kLoop, calls=%fused_computation.47 | loop fusion | flops 27262976 | bytes 12670976 | tf_op jit(solution)/shard_map/add | solution.py:291
  539.7 105.8 %all-reduce.10.cloned.1.call-done = f32[137,32,512]{2,1,0:T(8,128)} async-done(((f32[137,32,512]{2,1,0:T(8,128)}), f32[137,32,512]{2,1,0:T(8,128)}) %all-reduce.10.cloned.1.call-update) | async-done | bytes 8978448 | tf_op jit(solution)/shard_map/psum | solution.py:310
  645.5 9.1 %concatenate.67 = f32[138,32,512]{2,1,0:T(8,128)} pad(f32[137,32,512]{2,1,0:T(8,128)} %all-reduce.10.cloned.1.call-done, f32[]{:T(128)} %constant.46.clone.1), padding=0_1x0_0x0_0 | pad | bytes 18022404 | tf_op jit(solution)/shard_map/concatenate | solution.py:311
  654.6 4.5 gather_fusion.1
  659.1 5.5 multiply_subtract_fusion
  (266 shorter events, 66.6 us)
Async XLA Ops:
  7.2 638.3 %all-reduce.10.cloned.1.call-start = ((), (), s32[]{:S(2)}) async-start(), calls=%async_computation | async-start | bytes 17956864 | tf_op jit(solution)/shard_map/psum | solution.py:310
  9.7 26.1 %collective-permute-start = (bf16[27,32,512]{2,1,0:T(8,128)(2,1)}, bf16[27,32,512]{2,1,0:T(8,128)(2,1)}, u32[]{:S(2)}, u32[]{:S(2)}) collective-permute-start(bf16[27,32,512]{2,1,0:T(8,128)(2,1)} %convert_element_type.160), channel_id=1, source_target_pairs={{0,4},{4,0},{8,12},{12,8},{16,20},{20,16},{24,28},{28,24},{1,5},{5... | collective-permute-start | bytes 2654216 | tf_op jit(solution)/shard_map/ppermute | solution.py:35
  14.0 87.0 %collective-permute-start.3 = (bf16[2,3,512]{2,1,0:T(4,128)(2,1)}, bf16[2,3,512]{2,1,0:T(4,128)(2,1)}, u32[]{:S(2)}, u32[]{:S(2)}) collective-permute-start(bf16[2,3,512]{2,1,0:T(4,128)(2,1)} %get-tuple-element.55), channel_id=1, source_target_pairs={{0,1},{1,2},{2,3},{4,5},{5,6},{6,7},{8,9},{9,10},{10,11},{12,13},{... | collective-permute-start | bytes 18440 | tf_op jit(solution)/shard_map/ppermute | solution.py:48
  16.1 85.0 %collective-permute-start.4 = (bf16[2,3,512]{2,1,0:T(4,128)(2,1)}, bf16[2,3,512]{2,1,0:T(4,128)(2,1)}, u32[]{:S(2)}, u32[]{:S(2)}) collective-permute-start(bf16[2,3,512]{2,1,0:T(4,128)(2,1)} %get-tuple-element.54), channel_id=1, source_target_pairs={{1,0},{2,1},{3,2},{5,4},{6,5},{7,6},{9,8},{10,9},{11,10},{13,12},{... | collective-permute-start | bytes 18440 | tf_op jit(solution)/shard_map/ppermute | solution.py:51
  19.7 21.2 %copy-start.50 = (f32[320]{0:T(512)}, f32[320]{0:T(512)S(1)}, u32[]{:S(2)}) copy-start(f32[320]{0:T(512)S(1)} %get-tuple-element.75) | copy-start | bytes 3844
  19.7 21.3 %copy-start.52 = (f32[320]{0:T(512)}, f32[320]{0:T(512)S(1)}, u32[]{:S(2)}) copy-start(f32[320]{0:T(512)S(1)} %get-tuple-element.76) | copy-start | bytes 3844
  19.7 21.3 %copy-start.54 = (f32[320]{0:T(512)}, f32[320]{0:T(512)S(1)}, u32[]{:S(2)}) copy-start(f32[320]{0:T(512)S(1)} %get-tuple-element.77) | copy-start | bytes 3844
  19.7 21.3 %copy-start.56 = (f32[320]{0:T(512)}, f32[320]{0:T(512)S(1)}, u32[]{:S(2)}) copy-start(f32[320]{0:T(512)S(1)} %get-tuple-element.78) | copy-start | bytes 3844
  25.4 15.6 %copy-start.26 = (f32[2,1024]{1,0:T(2,128)}, f32[2,1024]{1,0:T(2,128)S(1)}, u32[]{:S(2)}) copy-start(f32[2,1024]{1,0:T(2,128)S(1)} %get-tuple-element.68) | copy-start | bytes 24580
  25.4 15.7 %copy-start.29 = (f32[2,1024]{1,0:T(2,128)}, f32[2,1024]{1,0:T(2,128)S(1)}, u32[]{:S(2)}) copy-start(f32[2,1024]{1,0:T(2,128)S(1)} %get-tuple-element.72) | copy-start | bytes 24580
  25.4 15.7 %copy-start.32 = (f32[2,1024]{1,0:T(2,128)}, f32[2,1024]{1,0:T(2,128)S(1)}, u32[]{:S(2)}) copy-start(f32[2,1024]{1,0:T(2,128)S(1)} %get-tuple-element.73) | copy-start | bytes 24580
  29.7 89.3 %collective-permute-start.6 = (f32[2,3,320]{1,2,0:T(8,128)}, f32[2,3,320]{1,2,0:T(8,128)}, u32[]{:S(2)}, u32[]{:S(2)}) collective-permute-start(f32[2,3,320]{1,2,0:T(8,128)} %slice.387), channel_id=1, source_target_pairs={{1,0},{2,1},{3,2},{5,4},{6,5},{7,6},{9,8},{10,9},{11,10},{13,12},{... | collective-permute-start | bytes 23048 | tf_op jit(solution)/shard_map/ppermute | solution.py:59
  33.6 6.3 copy-start.74
  38.3 39.7 %collective-permute-start.1 = (bf16[54,32,512]{2,1,0:T(8,128)(2,1)S(1)}, bf16[54,32,512]{2,1,0:T(8,128)(2,1)S(1)}, u32[]{:S(2)}, u32[]{:S(2)}) collective-permute-start(bf16[54,32,512]{2,1,0:T(8,128)(2,1)S(1)} %maximum_select_fusion.2), channel_id=1, source_target_pairs={{0,8},{4,12},{8,0},{12,4},{16,24},{20,28},{24,16},{28,20},{1,9},{5... | collective-permute-start | bytes 5308424 | tf_op jit(solution)/shard_map/ppermute | solution.py:35
  40.1 58.2 %copy-start.78 = (pred[137]{0:T(512)(128)(4,1)}, pred[137]{0:T(512)(128)(4,1)S(1)}, u32[]{:S(2)}) copy-start(pred[137]{0:T(512)(128)(4,1)S(1)} %get-tuple-element.36) | copy-start | bytes 415
  43.2 39.3 %copy-start.81 = (s32[2,4]{1,0:T(2,128)S(1)}, s32[2,4]{1,0:T(2,128)}, u32[]{:S(2)}) copy-start(s32[2,4]{1,0:T(2,128)} %param.10) | copy-start | bytes 100
  78.5 155.6 %collective-permute-start.2 = (bf16[108,32,512]{2,1,0:T(8,128)(2,1)S(1)}, bf16[108,32,512]{2,1,0:T(8,128)(2,1)}, u32[]{:S(2)}, u32[]{:S(2)}) collective-permute-start(bf16[108,32,512]{2,1,0:T(8,128)(2,1)S(1)} %maximum_select_fusion.1), channel_id=1, source_target_pairs={{0,16},{4,20},{8,24},{12,28},{16,0},{20,4},{24,8},{28,12},{1,17},{... | collective-permute-start | bytes 10616840 | tf_op jit(solution)/shard_map/ppermute | solution.py:35
  241.3 10.7 %copy-start.59 = (pred[4384]{0:T(1024)(128)(4,1)S(1)}, pred[4384]{0:T(1024)(128)(4,1)}, u32[]{:S(2)}) copy-start(pred[4384]{0:T(1024)(128)(4,1)} %broadcast_in_dim.52) | copy-start | bytes 13156
  256.2 14.7 %copy-start.15 = (bf16[4384,512]{1,0:T(8,128)(2,1)}, bf16[4384,512]{1,0:T(8,128)(2,1)S(1)}, u32[]{:S(2)}) copy-start(bf16[4384,512]{1,0:T(8,128)(2,1)S(1)} %bitcast_select_fusion) | copy-start | bytes 13467652
  256.3 5.3 slice-start
  259.0 8.6 %copy-start.60 = (f32[1,512]{1,0:T(1,128)}, f32[1,512]{1,0:T(1,128)S(1)}, u32[]{:S(2)}) copy-start(f32[1,512]{1,0:T(1,128)S(1)} %get-tuple-element.59) | copy-start | bytes 6148
  259.0 8.6 %copy-start.62 = (f32[1,512]{1,0:T(1,128)}, f32[1,512]{1,0:T(1,128)S(1)}, u32[]{:S(2)}) copy-start(f32[1,512]{1,0:T(1,128)S(1)} %get-tuple-element.60) | copy-start | bytes 6148
  259.0 8.6 %copy-start.64 = (f32[1,512]{1,0:T(1,128)}, f32[1,512]{1,0:T(1,128)S(1)}, u32[]{:S(2)}) copy-start(f32[1,512]{1,0:T(1,128)S(1)} %get-tuple-element.61) | copy-start | bytes 6148
  259.0 8.6 %copy-start.66 = (f32[1,512]{1,0:T(1,128)}, f32[1,512]{1,0:T(1,128)S(1)}, u32[]{:S(2)}) copy-start(f32[1,512]{1,0:T(1,128)S(1)} %get-tuple-element.62) | copy-start | bytes 6148
  259.0 8.6 %copy-start.68 = (f32[1,512]{1,0:T(1,128)}, f32[1,512]{1,0:T(1,128)S(1)}, u32[]{:S(2)}) copy-start(f32[1,512]{1,0:T(1,128)S(1)} %get-tuple-element.63) | copy-start | bytes 6148
  259.0 8.6 %copy-start.70 = (f32[1,512]{1,0:T(1,128)}, f32[1,512]{1,0:T(1,128)S(1)}, u32[]{:S(2)}) copy-start(f32[1,512]{1,0:T(1,128)S(1)} %get-tuple-element.64) | copy-start | bytes 6148
  259.1 8.6 %copy-start.72 = (f32[1,512]{1,0:T(1,128)}, f32[1,512]{1,0:T(1,128)S(1)}, u32[]{:S(2)}) copy-start(f32[1,512]{1,0:T(1,128)S(1)} %get-tuple-element.65) | copy-start | bytes 6148
  268.6 7.2 %copy-start.44 = (f32[2048]{0:T(1024)}, f32[2048]{0:T(1024)S(1)}, u32[]{:S(2)}) copy-start(f32[2048]{0:T(1024)S(1)} %bitcast_rsqrt_fusion) | copy-start | bytes 24580
  276.6 35.4 %copy-start.25 = (bf16[48,32,512]{2,1,0:T(8,128)(2,1)}, bf16[48,32,512]{2,1,0:T(8,128)(2,1)S(1)}, u32[]{:S(2)}) copy-start(bf16[48,32,512]{2,1,0:T(8,128)(2,1)S(1)} %get-tuple-element.45) | copy-start | bytes 4718596
  280.6 31.4 %copy-start.19 = (bf16[2048,512]{1,0:T(8,128)(2,1)}, bf16[2048,512]{1,0:T(8,128)(2,1)S(1)}, u32[]{:S(2)}) copy-start(bf16[2048,512]{1,0:T(8,128)(2,1)S(1)} %add_convert_fusion.3) | copy-start | bytes 6291460
  280.7 31.4 %copy-start.18 = (bf16[2,1024,512]{2,1,0:T(8,128)(2,1)S(1)}, bf16[2,1024,512]{2,1,0:T(8,128)(2,1)}, u32[]{:S(2)}) copy-start(bf16[2,1024,512]{2,1,0:T(8,128)(2,1)} %param.8) | copy-start | bytes 6291460
  312.1 5.6 copy-start.83
  366.4 5.6 copy-start.5
  372.0 16.5 %copy-start.4 = (f32[2048,512]{1,0:T(8,128)S(1)}, f32[2048,512]{1,0:T(8,128)}, u32[]{:S(2)}) copy-start(f32[2048,512]{1,0:T(8,128)} %bitcast_subtract_fusion) | copy-start | bytes 12582916
  372.0 16.5 %copy-start.6 = (f32[2048,512]{1,0:T(8,128)S(1)}, f32[2048,512]{1,0:T(8,128)}, u32[]{:S(2)}) copy-start(f32[2048,512]{1,0:T(8,128)} %fusion.60) | copy-start | bytes 12582916
  388.5 6.7 copy-start.20
  388.5 6.7 copy-start.82
  395.2 7.3 %copy-start.7 = (f32[2048,512]{1,0:T(8,128)}, f32[2048,512]{1,0:T(8,128)S(1)}, u32[]{:S(2)}) copy-start(f32[2048,512]{1,0:T(8,128)S(1)} %get-tuple-element.88) | copy-start | bytes 12582916
  410.3 8.6 %copy-start.2 = (f32[2048,512]{1,0:T(8,128)}, f32[2048,512]{1,0:T(8,128)S(1)}, u32[]{:S(2)}) copy-start(f32[2048,512]{1,0:T(8,128)S(1)} %get-tuple-element.25) | copy-start | bytes 12582916
  469.6 14.4 %copy-start.58 = (f32[4,320]{1,0:T(4,128)S(1)}, f32[4,320]{1,0:T(4,128)}, u32[]{:S(2)}) copy-start(f32[4,320]{1,0:T(4,128)} %multiply_subtract_fusion.2) | copy-start | bytes 15364
  495.1 14.9 %copy-start.51 = (f32[320]{0:T(512)S(1)}, f32[320]{0:T(512)}, u32[]{:S(2)}) copy-start(f32[320]{0:T(512)} %copy-done.50) | copy-start | bytes 3844
  495.1 14.9 %copy-start.53 = (f32[320]{0:T(512)S(1)}, f32[320]{0:T(512)}, u32[]{:S(2)}) copy-start(f32[320]{0:T(512)} %copy-done.52) | copy-start | bytes 3844
  495.1 14.9 %copy-start.55 = (f32[320]{0:T(512)S(1)}, f32[320]{0:T(512)}, u32[]{:S(2)}) copy-start(f32[320]{0:T(512)} %copy-done.54) | copy-start | bytes 3844
  495.1 14.9 %copy-start.57 = (f32[320]{0:T(512)S(1)}, f32[320]{0:T(512)}, u32[]{:S(2)}) copy-start(f32[320]{0:T(512)} %copy-done.56) | copy-start | bytes 3844
  495.2 14.8 %collective-permute-start.5 = (f32[2,3,320]{1,2,0:T(8,128)S(1)}, f32[2,3,320]{1,2,0:T(8,128)S(1)}, u32[]{:S(2)}, u32[]{:S(2)}) collective-permute-start(f32[2,3,320]{1,2,0:T(8,128)S(1)} %pad_add_fusion.1), channel_id=1, source_target_pairs={{0,1},{1,2},{2,3},{4,5},{5,6},{6,7},{8,9},{9,10},{10,11},{12,13},{... | collective-permute-start | bytes 23048 | tf_op jit(solution)/shard_map/ppermute | solution.py:59
  500.8 18.1 %collective-permute-start.7 = (f32[2,3,512]{2,1,0:T(4,128)S(1)}, f32[2,3,512]{2,1,0:T(4,128)S(1)}, u32[]{:S(2)}, u32[]{:S(2)}) collective-permute-start(f32[2,3,512]{2,1,0:T(4,128)S(1)} %get-tuple-element.49), channel_id=1, source_target_pairs={{1,0},{2,1},{3,2},{5,4},{6,5},{7,6},{9,8},{10,9},{11,10},{13,12},{... | collective-permute-start | bytes 36872 | tf_op jit(solution)/shard_map/ppermute | solution.py:51
  502.1 16.8 %collective-permute-start.8 = (f32[2,3,512]{2,1,0:T(4,128)S(1)}, f32[2,3,512]{2,1,0:T(4,128)S(1)}, u32[]{:S(2)}, u32[]{:S(2)}) collective-permute-start(f32[2,3,512]{2,1,0:T(4,128)S(1)} %get-tuple-element.50), channel_id=1, source_target_pairs={{0,1},{1,2},{2,3},{4,5},{5,6},{6,7},{8,9},{9,10},{10,11},{12,13},{... | collective-permute-start | bytes 36872 | tf_op jit(solution)/shard_map/ppermute | solution.py:48
  539.7 119.4 %copy-start.80 = (pred[27]{0:T(512)(128)(4,1)S(1)}, pred[27]{0:T(512)(128)(4,1)}, u32[]{:S(2)}) copy-start(pred[27]{0:T(512)(128)(4,1)} %get-tuple-element.18) | copy-start | bytes 85
  (52 other events, 199.7 us)
Sparse Core Ops, SparseCore 0:
  454.5 190.9 all-reduce.9
